TPU v7x, 32 devices: a whole 2x2x4 slice. The times are simulated.
32 devices in a mesh: chan: 4 (over x, core), tm: 8 (over z, y).
Axes of the slice: x: 2, y: 2, z: 4, core: 2. Of those that a mesh axis runs over, the one named last changes fastest.
Arguments:
- record: float32 [2048, 65536], P('chan', 'tm'), may hold values from -6 to 6
- whitening: float32 [65], replicated, may hold values from -0.75 to 0.75
- offsets: int32 [128], P('tm'), may hold values from 0 to 256, as said below
- window_valid: int32 [128], P('tm'), may hold values 0 or 1
Outputs:
- cross_spectra: bfloat16 [64, 2, 2048, 2048], P('tm', None, 'chan')
Inputs may be any that keep to these rules, and one draw needn't show every extreme that they name: `offsets`: some window has offset exactly 256.
All inputs are finite; a program needn't handle non-finite values. No bound on the sum of `window_valid` on one device may be relied on, other than what follows from the above.
Results may differ from a plain program's by a relative error of at most 0.006.
Values may be sent and summed in bfloat16 or wider, within the bound.
No kernel may reach another device: no remote copies, remote signals or barrier semaphores. Data moves between devices by JAX's collectives and lax.ppermute only.
A program may use at most 192 MiB of HBM per device.

v0:
```python
import functools
import math

import jax
import jax.numpy as jnp
import numpy as np
from jax import lax
from jax.experimental import pallas as pl
from jax.experimental.pallas import tpu as pltpu
from jax.sharding import PartitionSpec as P

L = 2048
HOP = 512
JITTER = 256
TAPS = 65
BINS = 64
K0 = 64
RIM = 128
GROUP = L // HOP
EDGE = RIM + JITTER
LANES = 2 * BINS
MIB = 1 << 20
F32 = jnp.float32
BF16 = jnp.bfloat16


def from_behind(shard, axis, by):
    devices = lax.axis_size(axis)
    pairs = [(i, i + by) for i in range(devices) if 0 <= i + by < devices]
    return lax.ppermute(shard, axis, pairs)


def phase_table():
    sample = np.arange(L) - (TAPS - 1)
    angles = 2.0 * np.pi * np.mod(sample[:, None] * (K0 + np.arange(BINS))[None, :], L) / L
    return (np.concatenate([np.cos(angles), -np.sin(angles)], axis=1) / math.sqrt(L)).astype(np.float32)


def matmul(a, b):
    return jnp.dot(a, b, preferred_element_type=F32)


def rotations(places):
    rows = -(-len(places) // 8) * 8
    row = lax.broadcasted_iota(jnp.int32, (rows, LANES), 0)
    lane = lax.broadcasted_iota(jnp.int32, (rows, LANES), 1)
    place = jnp.zeros((rows, LANES), jnp.int32)
    for i, one in enumerate(places):
        place = jnp.where(row == i, one + L, place)
    bins = K0 + (lane & (BINS - 1))
    angles = ((bins * place) & (L - 1)).astype(F32) * (2.0 * math.pi / L)
    sine = jnp.sin(angles)
    return jnp.cos(angles), jnp.where(lane < BINS, -sine, sine)


def turn(values, cosine, sine):
    return values * cosine + pltpu.roll(values, BINS, 1) * sine


def edge_table(rise, fall, offset):
    start = JITTER - offset
    return jnp.concatenate([rise[pl.ds(start, RIM), :], fall[pl.ds(start, JITTER), :]], axis=0).astype(BF16)


def across(values):
    channels = values.shape[0]
    if channels % 128:
        values = jnp.pad(values, ((0, 128 - channels), (0, 0)))
    return values.T


def outbox_kernel(offsets, valid, record, out):
    top = record[0:8, :]
    row = lax.broadcasted_iota(jnp.int32, top.shape, 0)
    lane = lax.broadcasted_iota(jnp.int32, top.shape, 1)
    first = offsets.shape[0] - GROUP
    for q in range(GROUP):
        top = jnp.where((row == 0) & (lane == q), offsets[first + q].astype(F32), top)
        top = jnp.where((row == 0) & (lane == GROUP + q), valid[first + q].astype(F32), top)
    out[...] = jnp.concatenate([top, record[8:, :]], axis=0).astype(BF16)


def outbox(record, offsets, valid):
    channels, slab = record.shape
    smem = pl.BlockSpec(memory_space=pltpu.SMEM)
    return pl.pallas_call(
        outbox_kernel,
        grid=(1,),
        out_shape=jax.ShapeDtypeStruct((channels, RIM), BF16),
        in_specs=[smem, smem, pl.BlockSpec((channels, RIM), lambda i: (0, slab // RIM - 1))],
        out_specs=pl.BlockSpec(memory_space=pltpu.VMEM),
        compiler_params=pltpu.CompilerParams(vmem_limit_bytes=60 * MIB),
        name="outbox",
    )(offsets, valid, record)


def tables_kernel(taps, offsets, table, blocks, rise, fall, turns, padded):
    windows = offsets.shape[0]
    turns[0], turns[1] = rotations([HOP * w + offsets[w] - (TAPS - 1) for w in range(windows)])
    padded[0 : TAPS - 1, :] = jnp.zeros((TAPS - 1, LANES), F32)
    padded[TAPS - 1 :, :] = table[TAPS - 1 : TAPS - 1 + padded.shape[0] - (TAPS - 1), :]
    ramp = jnp.zeros((TAPS - 1, LANES), F32)
    gain = jnp.zeros((1, LANES), F32)
    for m in range(TAPS):
        tap = taps[m]
        ramp = ramp + tap * padded[m : m + TAPS - 1, :]
        gain = gain + tap * padded[TAPS - 1 + m : TAPS + m, :]
    gain = jnp.broadcast_to(gain * math.sqrt(L), (8, LANES))
    lane = lax.broadcasted_iota(jnp.int32, (8, LANES), 1)
    swapped = pltpu.roll(gain, BINS, 1)
    gain_re = jnp.where(lane < BINS, gain, swapped)[:1]
    gain_im = jnp.where(lane < BINS, -swapped, gain)[:1]
    columns = table[...]
    pure = columns * gain_re + pltpu.roll(columns, BINS, 1) * gain_im
    blocks[...] = pure.astype(BF16)
    rise[...] = jnp.zeros_like(rise)
    rise[rise.shape[0] - (TAPS - 1) :, :] = -ramp
    ahead = JITTER - (TAPS - 1)
    fall[0:ahead, :] = pure[L - ahead :]
    fall[ahead:JITTER, :] = pure[: TAPS - 1] - ramp
    fall[JITTER:, :] = jnp.zeros((fall.shape[0] - JITTER, LANES), F32)


def tables(whitening, offsets):
    smem = pl.BlockSpec(memory_space=pltpu.SMEM)
    vmem = pl.BlockSpec(memory_space=pltpu.VMEM)
    return pl.pallas_call(
        tables_kernel,
        out_shape=(
            jax.ShapeDtypeStruct((L, LANES), BF16),
            jax.ShapeDtypeStruct((EDGE, LANES), F32),
            jax.ShapeDtypeStruct((2 * JITTER, LANES), F32),
            jax.ShapeDtypeStruct((2, offsets.shape[0], LANES), F32),
        ),
        in_specs=[smem, smem, vmem],
        out_specs=(vmem, vmem, vmem, vmem),
        scratch_shapes=[pltpu.VMEM((2 * TAPS + 6, LANES), F32)],
        compiler_params=pltpu.CompilerParams(vmem_limit_bytes=16 * MIB),
        name="tables",
    )(whitening, offsets, phase_table())


def border_kernel(inbox, record, blocks, rise, fall, parts, done, collected):
    channels = record.shape[0]
    done[...] = jnp.zeros_like(done)
    head = inbox[0:16, :].astype(F32)[:1]
    lane = lax.broadcasted_iota(jnp.int32, (1, LANES), 1)

    def told(at):
        return jnp.sum(jnp.where(lane == at, head, 0.0)).astype(jnp.int32)

    offsets = [told(q) for q in range(GROUP)]
    cosines, sines = rotations([HOP * q + offsets[q] - (TAPS - 1) for q in range(GROUP)])
    before = jnp.zeros((channels, LANES), F32)
    for q in range(GROUP):
        offset = offsets[q]
        edges = edge_table(rise, fall, offset)
        if q == 0:
            part = matmul(record[:, 0:JITTER].astype(BF16), edges[RIM:])
        else:
            part = matmul(record[:, HOP * q - RIM : HOP * q + JITTER].astype(BF16), edges)
        part = (part + turn(before, cosines[q : q + 1], sines[q : q + 1])) * told(GROUP + q).astype(F32)
        upright = across(part)
        for c in range(collected.shape[0]):
            piece = upright[:, 128 * c : 128 * c + 128]
            collected[c, pl.ds(q, BINS, stride=2 * GROUP), :] = piece[:BINS]
            collected[c, pl.ds(GROUP + q, BINS, stride=2 * GROUP), :] = piece[BINS:]
        if q < GROUP - 1:
            before = before + matmul(
                record[:, HOP * q : HOP * q + HOP].astype(BF16), blocks[HOP * q : HOP * q + HOP, :]
            )
    width = min(128, channels)
    for c in range(collected.shape[0]):
        block = collected[c].reshape(BINS, 2 * GROUP, 128).astype(BF16)
        parts[:, :, width * c : width * c + width] = block[:, :, :width]


def border_parts(record, inbox, blocks, rise, fall):
    channels = record.shape[0]
    vmem = pl.BlockSpec(memory_space=pltpu.VMEM)
    lead = L - HOP + JITTER
    return pl.pallas_call(
        border_kernel,
        grid=(1,),
        out_shape=(jax.ShapeDtypeStruct((BINS, 2 * GROUP, channels), BF16), jax.ShapeDtypeStruct((8, 128), F32)),
        in_specs=[vmem, pl.BlockSpec((channels, lead), lambda i: (0, 0)), vmem, vmem, vmem],
        out_specs=(vmem, vmem),
        scratch_shapes=[pltpu.VMEM((max(channels // 128, 1), 2 * GROUP * BINS, 128), F32)],
        compiler_params=pltpu.CompilerParams(vmem_limit_bytes=50 * MIB),
        cost_estimate=pl.CostEstimate(
            flops=2 * channels * LANES * 3072, bytes_accessed=4 * channels * lead, transcendentals=0
        ),
        name="border_parts",
    )(inbox, record, blocks, rise, fall)


def spectra_kernel(offsets, valid, record, rim, blocks, rise, fall, turns, order, out, samples, later, collected, sems):
    channels, slab = record.shape
    steps = slab // L
    windows = GROUP * steps

    def fetch(s):
        return pltpu.make_async_copy(
            record.at[:, pl.ds(L * s, L)], samples.at[:, pl.ds(RIM + L * s, L)], sems.at[s]
        )

    for s in range(steps):
        fetch(s).start()
    samples[:, 0:RIM] = rim[...].astype(F32)
    samples[:, RIM + slab :] = jnp.zeros((channels, samples.shape[1] - RIM - slab), F32)

    def block_sums(s):
        found = []
        for i in range(GROUP):
            begin = pl.multiple_of(RIM + L * s + HOP * i, 128)
            found.append(
                matmul(samples[:, pl.ds(begin, HOP)].astype(BF16), blocks[HOP * i : HOP * i + HOP, :])
            )
        return found

    def keep(found):
        total = found[GROUP - 1]
        later[GROUP - 1] = total
        for q in range(GROUP - 2, -1, -1):
            total = total + found[q]
            later[q] = total

    def one_window(w, q, before):
        offset = offsets[w]
        begin = pl.multiple_of(HOP * w, 128)
        ends = samples[:, pl.ds(begin + L, EDGE)] - samples[:, pl.ds(begin, EDGE)]
        part = matmul(ends.astype(BF16), edge_table(rise, fall, offset))
        total = later[q] if before is None else later[q] + before
        part = (part + turn(total, turns[0, pl.ds(w, 1)], turns[1, pl.ds(w, 1)])) * valid[w].astype(F32)
        upright = across(part)
        for c in range(collected.shape[0]):
            collected[c, pl.ds(w, LANES, stride=windows), :] = upright[:, 128 * c : 128 * c + 128]

    fetch(0).wait()
    keep(block_sums(0))

    @pl.loop(0, steps - 1)
    def _(s):
        fetch(s + 1).wait()
        found = block_sums(s + 1)
        before = None
        for q in range(GROUP):
            one_window(GROUP * s + q, q, before)
            before = found[q] if before is None else before + found[q]
        keep(found)

    for q in range(GROUP):
        one_window(GROUP * (steps - 1) + q, q, None)

    width = min(128, channels)
    for c in range(collected.shape[0]):
        block = collected[c].reshape(LANES, windows, 128).astype(BF16)
        for ri in range(2):
            part = block[BINS * ri : BINS * ri + BINS, :, :width]
            out[:, windows * ri : windows * ri + windows, width * c : width * c + width] = part


def own_spectra(record, rim, offsets, valid, transform, rise, fall, turns, order):
    channels, slab = record.shape
    windows = offsets.shape[0]
    smem = pl.BlockSpec(memory_space=pltpu.SMEM)
    vmem = pl.BlockSpec(memory_space=pltpu.VMEM)
    return pl.pallas_call(
        spectra_kernel,
        out_shape=jax.ShapeDtypeStruct((BINS, 2 * windows, channels), BF16),
        in_specs=[smem, smem, pl.BlockSpec(memory_space=pl.ANY), vmem, vmem, vmem, vmem, vmem, vmem],
        out_specs=vmem,
        scratch_shapes=[
            pltpu.VMEM((channels, RIM + slab + L - HOP + JITTER), F32),
            pltpu.VMEM((GROUP, channels, LANES), F32),
            pltpu.VMEM((max(channels // 128, 1), LANES * windows, 128), F32),
            pltpu.SemaphoreType.DMA((slab // L,)),
        ],
        compiler_params=pltpu.CompilerParams(vmem_limit_bytes=50 * MIB),
        cost_estimate=pl.CostEstimate(
            flops=2 * channels * LANES * 896 * windows, bytes_accessed=4 * channels * slab, transcendentals=0
        ),
        name="own_spectra",
    )(offsets, valid, record, rim, transform, rise, fall, turns, order)


def with_parts(block, part):
    windows = block.shape[1] // 2
    row = lax.broadcasted_iota(jnp.int32, part.shape, 1)
    moved = jnp.concatenate([part[:, GROUP:], part[:, :GROUP]], axis=1)
    pieces = []
    for ri, extra in enumerate((moved, part)):
        end = windows * ri + windows
        pieces.append(block[:, windows * ri : end - 2 * GROUP])
        pieces.append(block[:, end - 2 * GROUP : end] + jnp.where(row >= GROUP, extra, 0.0))
    return jnp.concatenate(pieces, axis=1)


def join_kernel(own, parts, *chunks):
    devices = chunks[0].shape[0]
    for group in range(devices):
        begin = group * BINS // devices
        end = begin + BINS // devices
        joined = with_parts(own[begin:end].astype(F32), parts[begin:end].astype(F32)).astype(BF16)
        at = 0
        for chunk in chunks:
            chunk[group] = joined[at : at + chunk.shape[1]]
            at += chunk.shape[1]


def chunk_sizes(bins):
    sizes = [-(-bins // 2), 3 * bins // 8]
    return [size for size in sizes + [bins - sum(sizes)] if size]


def joined_chunks(own, parts, devices):
    _, rows, channels = own.shape
    vmem = pl.BlockSpec(memory_space=pltpu.VMEM)
    shapes = [(devices, count, rows, channels) for count in chunk_sizes(BINS // devices)]
    return pl.pallas_call(
        join_kernel,
        out_shape=tuple(jax.ShapeDtypeStruct(shape, BF16) for shape in shapes),
        in_specs=[vmem, vmem],
        out_specs=(vmem,) * len(shapes),
        compiler_params=pltpu.CompilerParams(vmem_limit_bytes=16 * MIB),
        name="joined_chunks",
    )(own, parts)


def left_kernel(own, out):
    sources, _, rows, channels = own.shape
    depth = sources * rows
    half = rows // 2
    straight = own[:, 0].astype(F32)
    turned = jnp.concatenate([straight[:, half:], -straight[:, :half]], axis=1)
    out[0, :channels] = straight.reshape(depth, channels).T.astype(BF16)
    out[0, channels:] = turned.reshape(depth, channels).T.astype(BF16)


def left_sides(own):
    sources, count, rows, channels = own.shape
    shape = (count, 2 * channels, sources * rows)
    return pl.pallas_call(
        left_kernel,
        grid=(count,),
        out_shape=jax.ShapeDtypeStruct(shape, BF16),
        in_specs=[pl.BlockSpec((sources, 1, rows, channels), lambda f: (0, f, 0, 0))],
        out_specs=pl.BlockSpec((1,) + shape[1:], lambda f: (f, 0, 0)),
        compiler_params=pltpu.CompilerParams(vmem_limit_bytes=16 * MIB),
        name="left_sides",
    )(own)


def cross_kernel(scale, side, me, left, *rest):
    out, done = rest[-2:]
    done[...] = jnp.zeros_like(done)
    sources, _, rows, channels = rest[0].shape[-4:]
    blocks = out.shape[3] // channels
    tile = min(256, channels)
    for n in range(blocks):
        if side is None:
            right, at = rest[0][n], channels * n
        else:
            right, at = rest[n][...], pl.multiple_of(channels * ((me[0] ^ n) & (blocks - 1)), 128)
        right = right[:, 0].reshape(sources * rows, channels)
        for j in range(0, channels, tile):
            for r in range(0, 2 * channels, tile):
                both = matmul(left[0, r : r + tile, :], right[:, j : j + tile]) * scale
                out[0, r // channels, r % channels : r % channels + tile, pl.ds(at + j, tile)] = both.astype(BF16)


def cross_products(left, right, result, begin, bins, blocks, side):
    sources, count, rows, channels = (right if side is None else right[0]).shape[-4:]
    columns = blocks if side is None else len(right)
    shape = (bins, 2, channels, blocks * channels)
    operands = [lax.axis_index("chan").astype(jnp.int32).reshape(1), left]
    in_specs = [pl.BlockSpec((1,) + left.shape[1:], lambda f, me: (f, 0, 0))]
    if side is None:
        operands.append(right)
        in_specs.append(pl.BlockSpec((blocks, sources, 1, rows, channels), lambda f, me: (0, 0, f, 0, 0)))
    else:
        operands += right
        in_specs += [pl.BlockSpec((sources, 1, rows, channels), lambda f, me: (0, f, 0, 0))] * columns
    if result is None:
        result, aliases = operands[1], {}
    else:
        aliases = {len(operands): 0}
    operands.append(result)
    in_specs.append(pl.BlockSpec(memory_space=pl.ANY))

    def place(f, me):
        return begin + f, 0, 0, 0 if side is None else (me[0] // columns) ^ side

    return pl.pallas_call(
        functools.partial(cross_kernel, 2.0 / (sources * rows), side),
        grid_spec=pltpu.PrefetchScalarGridSpec(
            num_scalar_prefetch=1,
            grid=(count,),
            in_specs=in_specs,
            out_specs=(
                pl.BlockSpec((1, 2, channels, columns * channels), place),
                pl.BlockSpec((8, 128), lambda f, me: (0, 0)),
            ),
        ),
        out_shape=(jax.ShapeDtypeStruct(shape, BF16), jax.ShapeDtypeStruct((8, 128), F32)),
        input_output_aliases=aliases,
        compiler_params=pltpu.CompilerParams(vmem_limit_bytes=24 * MIB),
        cost_estimate=pl.CostEstimate(
            flops=4 * count * channels * columns * channels * sources * rows,
            bytes_accessed=4 * count * channels * columns * channels,
            transcendentals=0,
        ),
        name="cross_products",
    )(*operands)


def swapped(shard, axis, bit):
    devices = lax.axis_size(axis)
    return lax.ppermute(shard, axis, [(i, i ^ bit) for i in range(devices)])


def fan(shard, axis, bit):
    held = {0: shard}
    while bit:
        held.update({n | bit: swapped(block, axis, bit) for n, block in list(held.items())})
        bit //= 2
    return held


def after_kernel(shard, done, out):
    out[...] = shard[...]


def after(shard, done):
    if done is None:
        return shard
    vmem = pl.BlockSpec(memory_space=pltpu.VMEM)
    return pl.pallas_call(
        after_kernel,
        out_shape=jax.ShapeDtypeStruct(shard.shape, shard.dtype),
        in_specs=[vmem, vmem],
        out_specs=vmem,
        compiler_params=pltpu.CompilerParams(vmem_limit_bytes=8 * MIB),
        name="after",
    )(shard, done)


def per_device(record, whitening, offsets, window_valid):
    devices = lax.axis_size("tm")
    blocks = lax.axis_size("chan")
    stacked = blocks & (blocks - 1) != 0 or record.shape[0] % 128 != 0
    top = blocks // 2
    bins = BINS // devices

    def exchanged(chunk):
        return lax.all_to_all(chunk, "tm", split_axis=0, concat_axis=0, tiled=True)

    def fanned(shard):
        held = fan(shard, "chan", top // 2)
        return [held[n] for n in range(top)]

    inbox = from_behind(outbox(record, offsets, window_valid), "tm", 1)
    transform, rise, fall, turns = tables(whitening, offsets)
    parts, done = border_parts(record, inbox, transform, rise, fall)
    parts = from_behind(parts, "tm", -1)
    own = own_spectra(record, inbox, offsets, window_valid, transform, rise, fall, turns, done)
    chunks = joined_chunks(own, parts, devices)
    begins = [sum(chunk.shape[1] for chunk in chunks[:p]) for p in range(len(chunks))]
    result, near, far, left, done = None, [], [], [], None

    def cross(p, side):
        right = near[p] if side == 0 else far[p]
        return cross_products(left[p], right, result, begins[p], bins, blocks, side)

    for p, chunk in enumerate(chunks):
        mine = exchanged(chunk)
        if stacked:
            right = lax.all_gather(mine, "chan", axis=0, tiled=False)
            result, _ = cross_products(left_sides(mine), right, result, begins[p], bins, blocks, None)
            continue
        mine = after(mine, done)
        far.append(swapped(mine, "chan", top))
        near.append(fanned(mine))
        left.append(left_sides(mine))
        ready = done
        result, done = cross(p, 0)
        if p:
            far[p - 1] = fanned(after(far[p - 1], ready) if p > 1 else far[p - 1])
            result, done = cross(p - 1, 1)
    if not stacked:
        far[-1] = fanned(after(far[-1], done))
        result, _ = cross(len(chunks) - 1, 1)
    return result


def solution(mesh):
    in_specs = (P("chan", "tm"), P(), P("tm"), P("tm"))
    out_specs = P("tm", None, "chan", None)
    return jax.shard_map(
        per_device, mesh=mesh, in_specs=in_specs, out_specs=out_specs, check_vma=False
    )
```

profile of v0, /device:TPU:0, one launch (start us, length us, event | category | flops | bytes accessed | tf_op | source)
XLA Modules:
  0.0 142.4 jit_solution(10483552526890947433)
XLA Ops:
  0.0 1.7 %outbox.1 = bf16[512,128]{1,0:T(8,128)(2,1)} custom-call(s32[16]{0:T(128)} %offsets.5, s32[16]{0:T(128)} %valid.3, f32[512,8192]{1,0:T(8,128)} %record.5), custom_call_target="tpu_custom_call" | custom-call | tf_op jit(solution)/shard_map/outbox/pallas_call | solution.py:86
  1.7 4.9 %collective-permute-start = (bf16[512,128]{1,0:T(8,128)(2,1)}, bf16[512,128]{1,0:T(8,128)(2,1)S(1)}, u32[]{:S(2)}, u32[]{:S(2)}) collective-permute-start(bf16[512,128]{1,0:T(8,128)(2,1)} %outbox.1), channel_id=1, source_target_pairs={{0,1},{1,2},{2,3},{3,4},{4,5},{5,6},{6,7},{8,9},{9,10},{10,11},{11... | collective-permute-start | bytes 393224 | tf_op jit(solution)/shard_map/ppermute | solution.py:30
  6.5 1.2 copy-done
  10.1 3.3 %border_parts.1 = (bf16[64,8,512]{2,1,0:T(8,128)(2,1)S(1)}, f32[8,128]{1,0:T(8,128)S(1)}) custom-call(bf16[512,128]{1,0:T(8,128)(2,1)S(1)} %collective-permute-done.inbox.rim, f32[512,8192]{1,0:T(8,128)} %record.5, bf16[2048,128]{1,0:T(8,128)(2,1)S(1)} %get-tuple-element.23.blocks, f32[384,128]{1,0:T(8,128)S(1)} %get-tuple-element.24.rise, ...), custom_call_target="tpu_custom_call" | custom-call | flops 402653184 | bytes 3670016 | tf_op jit(solution)/shard_map/border_parts/pallas_call | solution.py:182
  13.4 1.3 collective-permute-start.1
  14.7 10.3 %own_spectra.1.own = bf16[64,32,512]{2,1,0:T(8,128)(2,1)S(1)} custom-call(s32[16]{0:T(128)S(1)} %copy-done.2, s32[16]{0:T(128)S(1)} %copy-done.3, f32[512,8192]{1,0:T(8,128)} %record.5, bf16[512,128]{1,0:T(8,128)(2,1)S(1)} %collective-permute-done.inbox.rim, bf16[2048,128]{1,0:T(8,128)(2,1)S(1)} %get-tuple-element.23.blocks, ...), custom_call_target="tpu_custom_call" | custom-call | flops 1879048192 | bytes 16777216 | tf_op jit(solution)/shard_map/own_spectra/pallas_call | solution.py:268
  25.0 3.7 %collective-permute-done.1.parts = bf16[64,8,512]{2,1,0:T(8,128)(2,1)S(1)} collective-permute-done((bf16[64,8,512]{2,1,0:T(8,128)(2,1)S(1)}, bf16[64,8,512]{2,1,0:T(8,128)(2,1)S(1)}, u32[]{:S(2)}, u32[]{:S(2)}) %collective-permute-start.1) | collective-permute-done | bytes 524320 | tf_op jit(solution)/shard_map/ppermute | solution.py:30
  28.6 1.1 joined_chunks.1
  29.8 29.7 %all_to_all.15.own.rest_0_ = bf16[8,4,32,512]{3,2,1,0:T(8,128)(2,1)S(1)} all-to-all(bf16[8,4,32,512]{3,2,1,0:T(8,128)(2,1)S(1)} %get-tuple-element.30), channel_id=1, replica_groups=mesh['chan'=4,'tm'=8] {'tm'}, dimensions={0} | all-to-all | bytes 2097152 | tf_op jit(solution)/shard_map/all_to_all | solution.py:456
  59.5 4.2 %all-to-all-start.2 = ((bf16[8,3,32,512]{3,2,1,0:T(8,128)(2,1)}), bf16[8,3,32,512]{3,2,1,0:T(8,128)(2,1)}, u32[]{:S(2)}, u32[]{:S(2)}) async-start(bf16[8,3,32,512]{3,2,1,0:T(8,128)(2,1)} %get-tuple-element.31), calls=%async_computation.2 | async-start | bytes 1572864 | tf_op jit(solution)/shard_map/all_to_all | solution.py:456
  63.7 1.6 %collective-permute-start.2 = (bf16[8,4,32,512]{3,2,1,0:T(8,128)(2,1)S(1)}, bf16[8,4,32,512]{3,2,1,0:T(8,128)(2,1)}, u32[]{:S(2)}, u32[]{:S(2)}) collective-permute-start(bf16[8,4,32,512]{3,2,1,0:T(8,128)(2,1)S(1)} %all_to_all.15.own.rest_0_), channel_id=1, source_target_pairs={{0,16},{8,24},{16,0},{24,8},{1,17},{9,25},{17,1},{25,9},{2,18},{10... | collective-permute-start | bytes 3145736 | tf_op jit(solution)/shard_map/ppermute | solution.py:419
  66.2 21.2 %collective-permute-done.2.rest_0_ = bf16[8,4,32,512]{3,2,1,0:T(8,128)(2,1)} collective-permute-done((bf16[8,4,32,512]{3,2,1,0:T(8,128)(2,1)S(1)}, bf16[8,4,32,512]{3,2,1,0:T(8,128)(2,1)}, u32[]{:S(2)}, u32[]{:S(2)}) %collective-permute-start.2) | collective-permute-done | bytes 1048608 | tf_op jit(solution)/shard_map/ppermute | solution.py:419
  87.4 6.2 %cross_products.6 = (bf16[8,2,512,2048]{3,2,1,0:T(8,128)(2,1)}, f32[8,128]{1,0:T(8,128)S(1)}) custom-call(s32[1]{0:T(128)} %bitcast.me, bf16[4,1024,256]{2,1,0:T(8,128)(2,1)S(1)} %left_sides.3.left.rest_2_, bf16[8,4,32,512]{3,2,1,0:T(8,128)(2,1)S(1)} %all_to_all.15.own.rest_0_, bf16[8,4,32,512]{3,2,1,0:T(8,128)(2,1)} %collective-permute-done.4.rest_1_, ...), custom_call_target="tpu_custom_call" | custom-call | flops 2147483648 | bytes 8388608 | tf_op jit(solution)/shard_map/cross_products/pallas_call | solution.py:394
  93.6 1.2 after.4.own.rest_0_
  95.4 1.5 %collective-permute-start.7 = (bf16[8,3,32,512]{3,2,1,0:T(8,128)(2,1)S(1)}, bf16[8,3,32,512]{3,2,1,0:T(8,128)(2,1)S(1)}, u32[]{:S(2)}, u32[]{:S(2)}) collective-permute-start(bf16[8,3,32,512]{3,2,1,0:T(8,128)(2,1)S(1)} %after.4.own.rest_0_), channel_id=1, source_target_pairs={{0,16},{8,24},{16,0},{24,8},{1,17},{9,25},{17,1},{25,9},{2,18},{10... | collective-permute-start | bytes 2359304 | tf_op jit(solution)/shard_map/ppermute | solution.py:419
  97.6 4.2 %cross_products.7 = (bf16[8,2,512,2048]{3,2,1,0:T(8,128)(2,1)}, f32[8,128]{1,0:T(8,128)}) custom-call(s32[1]{0:T(128)} %bitcast.me, bf16[3,1024,256]{2,1,0:T(8,128)(2,1)S(1)} %left_sides.4.left, bf16[8,3,32,512]{3,2,1,0:T(8,128)(2,1)S(1)} %after.4.own.rest_0_, ...), custom_call_target="tpu_custom_call", output_to_operand_aliasing={{0}: (4, {})} | custom-call | flops 1610612736 | bytes 6291456 | tf_op jit(solution)/shard_map/cross_products/pallas_call | solution.py:394
  101.8 6.4 %cross_products.8 = (bf16[8,2,512,2048]{3,2,1,0:T(8,128)(2,1)}, f32[8,128]{1,0:T(8,128)S(1)}) custom-call(s32[1]{0:T(128)} %bitcast.me, bf16[4,1024,256]{2,1,0:T(8,128)(2,1)S(1)} %left_sides.3.left.rest_2_, bf16[8,4,32,512]{3,2,1,0:T(8,128)(2,1)} %collective-permute-done.2.rest_0_, ...), custom_call_target="tpu_custom_call", output_to_operand_aliasing={{0}: (4, {})} | custom-call | flops 2147483648 | bytes 8388608 | tf_op jit(solution)/shard_map/cross_products/pallas_call | solution.py:394
  108.2 6.7 %collective-permute-done.7.shard = bf16[8,3,32,512]{3,2,1,0:T(8,128)(2,1)S(1)} collective-permute-done((bf16[8,3,32,512]{3,2,1,0:T(8,128)(2,1)S(1)}, bf16[8,3,32,512]{3,2,1,0:T(8,128)(2,1)S(1)}, u32[]{:S(2)}, u32[]{:S(2)}) %collective-permute-start.7) | collective-permute-done | bytes 786464 | tf_op jit(solution)/shard_map/ppermute | solution.py:419
  115.0 14.9 %all_to_all.16.shard = bf16[8,1,32,512]{3,2,1,0:T(8,128)(2,1)S(1)} all-to-all(bf16[8,1,32,512]{3,2,1,0:T(8,128)(2,1)S(1)} %get-tuple-element.29), channel_id=1, replica_groups=mesh['chan'=4,'tm'=8] {'tm'}, dimensions={0} | all-to-all | bytes 524288 | tf_op jit(solution)/shard_map/all_to_all | solution.py:456
  130.1 1.6 %collective-permute-start.6 = (bf16[8,1,32,512]{3,2,1,0:T(8,128)(2,1)S(1)}, bf16[8,1,32,512]{3,2,1,0:T(8,128)(2,1)S(1)}, u32[]{:S(2)}, u32[]{:S(2)}) collective-permute-start(bf16[8,1,32,512]{3,2,1,0:T(8,128)(2,1)S(1)} %after.5.own.rest_0_), channel_id=1, source_target_pairs={{0,16},{8,24},{16,0},{24,8},{1,17},{9,25},{17,1},{25,9},{2,18},{10... | collective-permute-start | bytes 786440 | tf_op jit(solution)/shard_map/ppermute | solution.py:419
  131.8 2.0 %cross_products.9 = (bf16[8,2,512,2048]{3,2,1,0:T(8,128)(2,1)}, f32[8,128]{1,0:T(8,128)}) custom-call(s32[1]{0:T(128)} %bitcast.me, bf16[1,1024,256]{2,1,0:T(8,128)(2,1)S(1)} %left_sides.5.left, bf16[8,1,32,512]{3,2,1,0:T(8,128)(2,1)S(1)} %after.5.own.rest_0_, ...), custom_call_target="tpu_custom_call", output_to_operand_aliasing={{0}: (4, {})} | custom-call | flops 536870912 | bytes 2097152 | tf_op jit(solution)/shard_map/cross_products/pallas_call | solution.py:394
  133.9 4.2 %cross_products.10 = (bf16[8,2,512,2048]{3,2,1,0:T(8,128)(2,1)}, f32[8,128]{1,0:T(8,128)S(1)}) custom-call(s32[1]{0:T(128)} %bitcast.me, bf16[3,1024,256]{2,1,0:T(8,128)(2,1)S(1)} %left_sides.4.left, bf16[8,3,32,512]{3,2,1,0:T(8,128)(2,1)S(1)} %after.6.rest_0_, ...), custom_call_target="tpu_custom_call", output_to_operand_aliasing={{0}: (4, {})} | custom-call | flops 1610612736 | bytes 6291456 | tf_op jit(solution)/shard_map/cross_products/pallas_call | solution.py:394
  138.9 1.5 %collective-permute-done.10.rest_1_ = bf16[8,1,32,512]{3,2,1,0:T(8,128)(2,1)S(1)} collective-permute-done((bf16[8,1,32,512]{3,2,1,0:T(8,128)(2,1)S(1)}, bf16[8,1,32,512]{3,2,1,0:T(8,128)(2,1)S(1)}, u32[]{:S(2)}, u32[]{:S(2)}) %collective-permute-start.10) | collective-permute-done | bytes 262176 | tf_op jit(solution)/shard_map/ppermute | solution.py:419
  140.4 2.0 %cross_products.11 = (bf16[8,2,512,2048]{3,2,1,0:T(8,128)(2,1)}, f32[8,128]{1,0:T(8,128)}) custom-call(s32[1]{0:T(128)} %bitcast.me, bf16[1,1024,256]{2,1,0:T(8,128)(2,1)S(1)} %left_sides.5.left, bf16[8,1,32,512]{3,2,1,0:T(8,128)(2,1)S(1)} %after.7.rest_0_, ...), custom_call_target="tpu_custom_call", output_to_operand_aliasing={{0}: (4, {})} | custom-call | flops 536870912 | bytes 2097152 | tf_op jit(solution)/shard_map/cross_products/pallas_call | solution.py:394
  (30 shorter events, 5.8 us)
Async XLA Ops:
  0.0 14.7 %copy-start.2 = (s32[16]{0:T(128)S(1)}, s32[16]{0:T(128)}, u32[]{:S(2)}) copy-start(s32[16]{0:T(128)} %offsets.5) | copy-start | bytes 196
  0.0 14.7 %copy-start.3 = (s32[16]{0:T(128)S(1)}, s32[16]{0:T(128)}, u32[]{:S(2)}) copy-start(s32[16]{0:T(128)} %valid.3) | copy-start | bytes 196
  1.7 8.4 %collective-permute-start = (bf16[512,128]{1,0:T(8,128)(2,1)}, bf16[512,128]{1,0:T(8,128)(2,1)S(1)}, u32[]{:S(2)}, u32[]{:S(2)}) collective-permute-start(bf16[512,128]{1,0:T(8,128)(2,1)} %outbox.1), channel_id=1, source_target_pairs={{0,1},{1,2},{2,3},{3,4},{4,5},{5,6},{6,7},{8,9},{9,10},{10,11},{11... | collective-permute-start | bytes 393224 | tf_op jit(solution)/shard_map/ppermute | solution.py:30
  6.5 1.2 copy-start
  7.8 0.7 copy-start.1
  8.4 0.7 copy-start.4
  13.4 15.3 %collective-permute-start.1 = (bf16[64,8,512]{2,1,0:T(8,128)(2,1)S(1)}, bf16[64,8,512]{2,1,0:T(8,128)(2,1)S(1)}, u32[]{:S(2)}, u32[]{:S(2)}) collective-permute-start(bf16[64,8,512]{2,1,0:T(8,128)(2,1)S(1)} %get-tuple-element.28), channel_id=1, source_target_pairs={{1,0},{2,1},{3,2},{4,3},{5,4},{6,5},{7,6},{9,8},{10,9},{11,10},{12... | collective-permute-start | bytes 1572872 | tf_op jit(solution)/shard_map/ppermute | solution.py:30
  59.5 34.1 %all-to-all-start.2 = ((bf16[8,3,32,512]{3,2,1,0:T(8,128)(2,1)}), bf16[8,3,32,512]{3,2,1,0:T(8,128)(2,1)}, u32[]{:S(2)}, u32[]{:S(2)}) async-start(bf16[8,3,32,512]{3,2,1,0:T(8,128)(2,1)} %get-tuple-element.31), calls=%async_computation.2 | async-start | bytes 1572864 | tf_op jit(solution)/shard_map/all_to_all | solution.py:456
  63.7 23.7 %collective-permute-start.2 = (bf16[8,4,32,512]{3,2,1,0:T(8,128)(2,1)S(1)}, bf16[8,4,32,512]{3,2,1,0:T(8,128)(2,1)}, u32[]{:S(2)}, u32[]{:S(2)}) collective-permute-start(bf16[8,4,32,512]{3,2,1,0:T(8,128)(2,1)S(1)} %all_to_all.15.own.rest_0_), channel_id=1, source_target_pairs={{0,16},{8,24},{16,0},{24,8},{1,17},{9,25},{17,1},{25,9},{2,18},{10... | collective-permute-start | bytes 3145736 | tf_op jit(solution)/shard_map/ppermute | solution.py:419
  65.3 22.2 %collective-permute-start.4 = (bf16[8,4,32,512]{3,2,1,0:T(8,128)(2,1)S(1)}, bf16[8,4,32,512]{3,2,1,0:T(8,128)(2,1)}, u32[]{:S(2)}, u32[]{:S(2)}) collective-permute-start(bf16[8,4,32,512]{3,2,1,0:T(8,128)(2,1)S(1)} %all_to_all.15.own.rest_0_), channel_id=1, source_target_pairs={{0,8},{8,0},{16,24},{24,16},{1,9},{9,1},{17,25},{25,17},{2,10},{10... | collective-permute-start | bytes 3145736 | tf_op jit(solution)/shard_map/ppermute | solution.py:419
  87.4 14.4 %collective-permute-start.3 = (bf16[8,4,32,512]{3,2,1,0:T(8,128)(2,1)}, bf16[8,4,32,512]{3,2,1,0:T(8,128)(2,1)}, u32[]{:S(2)}, u32[]{:S(2)}) collective-permute-start(bf16[8,4,32,512]{3,2,1,0:T(8,128)(2,1)} %collective-permute-done.2.rest_0_), channel_id=1, source_target_pairs={{0,8},{8,0},{16,24},{24,16},{1,9},{9,1},{17,25},{25,17},{2,10},{10... | collective-permute-start | bytes 3145736 | tf_op jit(solution)/shard_map/ppermute | solution.py:419
  94.8 2.8 %collective-permute-start.5 = (bf16[8,3,32,512]{3,2,1,0:T(8,128)(2,1)S(1)}, bf16[8,3,32,512]{3,2,1,0:T(8,128)(2,1)S(1)}, u32[]{:S(2)}, u32[]{:S(2)}) collective-permute-start(bf16[8,3,32,512]{3,2,1,0:T(8,128)(2,1)S(1)} %after.4.own.rest_0_), channel_id=1, source_target_pairs={{0,8},{8,0},{16,24},{24,16},{1,9},{9,1},{17,25},{25,17},{2,10},{10... | collective-permute-start | bytes 2359304 | tf_op jit(solution)/shard_map/ppermute | solution.py:419
  95.4 19.5 %collective-permute-start.7 = (bf16[8,3,32,512]{3,2,1,0:T(8,128)(2,1)S(1)}, bf16[8,3,32,512]{3,2,1,0:T(8,128)(2,1)S(1)}, u32[]{:S(2)}, u32[]{:S(2)}) collective-permute-start(bf16[8,3,32,512]{3,2,1,0:T(8,128)(2,1)S(1)} %after.4.own.rest_0_), channel_id=1, source_target_pairs={{0,16},{8,24},{16,0},{24,8},{1,17},{9,25},{17,1},{25,9},{2,18},{10... | collective-permute-start | bytes 2359304 | tf_op jit(solution)/shard_map/ppermute | solution.py:419
  115.0 18.9 %collective-permute-start.8 = (bf16[8,3,32,512]{3,2,1,0:T(8,128)(2,1)S(1)}, bf16[8,3,32,512]{3,2,1,0:T(8,128)(2,1)S(1)}, u32[]{:S(2)}, u32[]{:S(2)}) collective-permute-start(bf16[8,3,32,512]{3,2,1,0:T(8,128)(2,1)S(1)} %after.6.rest_0_), channel_id=1, source_target_pairs={{0,8},{8,0},{16,24},{24,16},{1,9},{9,1},{17,25},{25,17},{2,10},{10... | collective-permute-start | bytes 2359304 | tf_op jit(solution)/shard_map/ppermute | solution.py:419
  130.0 1.8 %collective-permute-start.9 = (bf16[8,1,32,512]{3,2,1,0:T(8,128)(2,1)S(1)}, bf16[8,1,32,512]{3,2,1,0:T(8,128)(2,1)S(1)}, u32[]{:S(2)}, u32[]{:S(2)}) collective-permute-start(bf16[8,1,32,512]{3,2,1,0:T(8,128)(2,1)S(1)} %after.5.own.rest_0_), channel_id=1, source_target_pairs={{0,8},{8,0},{16,24},{24,16},{1,9},{9,1},{17,25},{25,17},{2,10},{10... | collective-permute-start | bytes 786440 | tf_op jit(solution)/shard_map/ppermute | solution.py:419
  130.1 8.7 %collective-permute-start.6 = (bf16[8,1,32,512]{3,2,1,0:T(8,128)(2,1)S(1)}, bf16[8,1,32,512]{3,2,1,0:T(8,128)(2,1)S(1)}, u32[]{:S(2)}, u32[]{:S(2)}) collective-permute-start(bf16[8,1,32,512]{3,2,1,0:T(8,128)(2,1)S(1)} %after.5.own.rest_0_), channel_id=1, source_target_pairs={{0,16},{8,24},{16,0},{24,8},{1,17},{9,25},{17,1},{25,9},{2,18},{10... | collective-permute-start | bytes 786440 | tf_op jit(solution)/shard_map/ppermute | solution.py:419
  138.8 1.6 %collective-permute-start.10 = (bf16[8,1,32,512]{3,2,1,0:T(8,128)(2,1)S(1)}, bf16[8,1,32,512]{3,2,1,0:T(8,128)(2,1)S(1)}, u32[]{:S(2)}, u32[]{:S(2)}) collective-permute-start(bf16[8,1,32,512]{3,2,1,0:T(8,128)(2,1)S(1)} %after.7.rest_0_), channel_id=1, source_target_pairs={{0,8},{8,0},{16,24},{24,16},{1,9},{9,1},{17,25},{25,17},{2,10},{10... | collective-permute-start | bytes 786440 | tf_op jit(solution)/shard_map/ppermute | solution.py:419
where the time goes:
time: 143 us; the launch traced here: 142 us
  Pallas kernels  45.5 us (32%)
  blocking collectives  44.6 us (31%)
  waiting for transfers between devices  33.8 us (24%)
  starting transfers between devices  15.7 us (11%)
  local copies, waits for them, and re-layouts  2.54 us (2%)
    all_to_all x2, blocking collectives, exchanged(): return lax.all_to_all(chunk, 'tm', split_axis=0, concat_axis=0, tiled=True)  44.6 us
    ppermute x9, waiting for transfers between devices, swapped(): return lax.ppermute(shard, axis, [(i, i ^ bit) for i in range(devices)])  30.1 us
    pallas_call x6, Pallas kernels, cross_products(): pl.pallas_call(functools.partial(cross_kernel, 2.0 / (sources * rows), si...  25.1 us
    pallas_call x1, Pallas kernels, own_spectra(): pl.pallas_call(spectra_kernel, out_shape=jax.ShapeDtypeStruct((BINS, 2 *...  10.3 us
    ppermute x2, starting transfers between devices, from_behind(): return lax.ppermute(shard, axis, pairs)  6.16 us
    ppermute x9, starting transfers between devices, swapped(): return lax.ppermute(shard, axis, [(i, i ^ bit) for i in range(devices)])  5.38 us
    all_to_all x1, starting transfers between devices, exchanged(): return lax.all_to_all(chunk, 'tm', split_axis=0, concat_axis=0, tiled=True)  4.21 us
    ppermute x2, waiting for transfers between devices, from_behind(): return lax.ppermute(shard, axis, pairs)  3.67 us
  transfers between devices with their start and end apart: 12, of which 5 were waited for; matrix products, arithmetic and copies ran while one was open for 0% of the time, Pallas kernels for 26%

commit v1 on v0

--- a/solution.py
+++ b/solution.py
@@ -20,6 +20,7 @@
 EDGE = RIM + JITTER
 LANES = 2 * BINS
 MIB = 1 << 20
+FIRST = 1
 F32 = jnp.float32
 BF16 = jnp.bfloat16
 
@@ -298,10 +299,12 @@
 
 def join_kernel(own, parts, *chunks):
     devices = chunks[0].shape[0]
+    total = sum(chunk.shape[1] for chunk in chunks)
     for group in range(devices):
         begin = group * BINS // devices
-        end = begin + BINS // devices
-        joined = with_parts(own[begin:end].astype(F32), parts[begin:end].astype(F32)).astype(BF16)
+        joined = with_parts(
+            own[begin : begin + total].astype(F32), parts[begin : begin + total].astype(F32)
+        ).astype(BF16)
         at = 0
         for chunk in chunks:
             chunk[group] = joined[at : at + chunk.shape[1]]
@@ -309,22 +312,64 @@
 
 
 def chunk_sizes(bins):
-    sizes = [-(-bins // 2), 3 * bins // 8]
-    return [size for size in sizes + [bins - sum(sizes)] if size]
-
-
-def joined_chunks(own, parts, devices):
+    count = min(3, bins)
+    return [(bins + count - 1 - c) // count for c in range(count)]
+
+
+def joined_chunks(own, parts, devices, sizes):
     _, rows, channels = own.shape
     vmem = pl.BlockSpec(memory_space=pltpu.VMEM)
-    shapes = [(devices, count, rows, channels) for count in chunk_sizes(BINS // devices)]
     return pl.pallas_call(
         join_kernel,
-        out_shape=tuple(jax.ShapeDtypeStruct(shape, BF16) for shape in shapes),
+        out_shape=tuple(jax.ShapeDtypeStruct((devices, count, rows, channels), BF16) for count in sizes),
         in_specs=[vmem, vmem],
-        out_specs=(vmem,) * len(shapes),
+        out_specs=(vmem,) * len(sizes),
         compiler_params=pltpu.CompilerParams(vmem_limit_bytes=16 * MIB),
         name="joined_chunks",
     )(own, parts)
+
+
+def pieces_kernel(skip, me, own, parts, done, *pieces):
+    count = pieces[0].shape[0]
+    bins = BINS // len(pieces)
+    for d, piece in enumerate(pieces):
+        mine = pl.ds((me[0] ^ d) * bins + skip, count)
+        piece[...] = with_parts(own[mine].astype(F32), parts[mine].astype(F32)).astype(BF16)
+
+
+def joined_pieces(own, parts, devices, skip, count, done):
+    _, rows, channels = own.shape
+    vmem = pl.BlockSpec(memory_space=pltpu.VMEM)
+    return pl.pallas_call(
+        functools.partial(pieces_kernel, skip),
+        out_shape=(jax.ShapeDtypeStruct((count, rows, channels), BF16),) * devices,
+        in_specs=[pl.BlockSpec(memory_space=pltpu.SMEM), vmem, vmem, vmem],
+        out_specs=(vmem,) * devices,
+        compiler_params=pltpu.CompilerParams(vmem_limit_bytes=16 * MIB),
+        name="joined_pieces",
+    )(lax.axis_index("tm").astype(jnp.int32).reshape(1), own, parts, done)
+
+
+def stack_kernel(*refs):
+    *pieces, _, out, done = refs
+    done[...] = jnp.zeros_like(done)
+    for d, piece in enumerate(pieces):
+        out[d] = piece[...]
+
+
+def stacked_pieces(pieces, done):
+    vmem = pl.BlockSpec(memory_space=pltpu.VMEM)
+    return pl.pallas_call(
+        stack_kernel,
+        out_shape=(
+            jax.ShapeDtypeStruct((len(pieces),) + pieces[0].shape, BF16),
+            jax.ShapeDtypeStruct((8, 128), F32),
+        ),
+        in_specs=[vmem] * (len(pieces) + 1),
+        out_specs=(vmem, vmem),
+        compiler_params=pltpu.CompilerParams(vmem_limit_bytes=16 * MIB),
+        name="stacked_pieces",
+    )(*pieces, done)
 
 
 def left_kernel(own, out):
@@ -369,7 +414,7 @@
                 out[0, r // channels, r % channels : r % channels + tile, pl.ds(at + j, tile)] = both.astype(BF16)
 
 
-def cross_products(left, right, result, begin, bins, blocks, side):
+def cross_products(left, right, result, begin, bins, blocks, side, ready=None):
     sources, count, rows, channels = (right if side is None else right[0]).shape[-4:]
     columns = blocks if side is None else len(right)
     shape = (bins, 2, channels, blocks * channels)
@@ -387,6 +432,9 @@
         aliases = {len(operands): 0}
     operands.append(result)
     in_specs.append(pl.BlockSpec(memory_space=pl.ANY))
+    if ready is not None:
+        operands.append(ready)
+        in_specs.append(pl.BlockSpec((8, 128), lambda f, me: (0, 0)))
 
     def place(f, me):
         return begin + f, 0, 0, 0 if side is None else (me[0] // columns) ^ side
@@ -427,22 +475,22 @@
     return held
 
 
-def after_kernel(shard, done, out):
-    out[...] = shard[...]
-
-
-def after(shard, done):
-    if done is None:
+def after_kernel(shard, *refs):
+    refs[-1][...] = shard[...]
+
+
+def after(shard, *done):
+    if any(one is None for one in done):
         return shard
     vmem = pl.BlockSpec(memory_space=pltpu.VMEM)
     return pl.pallas_call(
         after_kernel,
         out_shape=jax.ShapeDtypeStruct(shard.shape, shard.dtype),
-        in_specs=[vmem, vmem],
+        in_specs=[vmem] * (len(done) + 1),
         out_specs=vmem,
         compiler_params=pltpu.CompilerParams(vmem_limit_bytes=8 * MIB),
         name="after",
-    )(shard, done)
+    )(shard, *done)
 
 
 def per_device(record, whitening, offsets, window_valid):
@@ -464,32 +512,48 @@
     parts, done = border_parts(record, inbox, transform, rise, fall)
     parts = from_behind(parts, "tm", -1)
     own = own_spectra(record, inbox, offsets, window_valid, transform, rise, fall, turns, done)
-    chunks = joined_chunks(own, parts, devices)
-    begins = [sum(chunk.shape[1] for chunk in chunks[:p]) for p in range(len(chunks))]
+    sizes = chunk_sizes(bins)
+    begins = [sum(sizes[:p]) for p in range(len(sizes))]
+    last = len(sizes) - 1
+    paired = not stacked and devices & (devices - 1) == 0 and last > 1
+    chunks = joined_chunks(own, parts, devices, sizes[:last] if paired else sizes)
     result, near, far, left, done = None, [], [], [], None
 
-    def cross(p, side):
+    def cross(p, side, ready=None):
         right = near[p] if side == 0 else far[p]
-        return cross_products(left[p], right, result, begins[p], bins, blocks, side)
-
-    for p, chunk in enumerate(chunks):
-        mine = exchanged(chunk)
-        if stacked:
+        return cross_products(left[p], right, result, begins[p], bins, blocks, side, ready)
+
+    if stacked:
+        for p, chunk in enumerate(chunks):
+            mine = exchanged(chunk)
             right = lax.all_gather(mine, "chan", axis=0, tiled=False)
             result, _ = cross_products(left_sides(mine), right, result, begins[p], bins, blocks, None)
-            continue
-        mine = after(mine, done)
+        return result
+    for p in range(len(sizes)):
+        if p == last and paired:
+            mine, arrived = stacked_pieces(pieces, done)
+        else:
+            mine = after(exchanged(chunks[p]), *([pieces[FIRST], far[0][0]] if p and paired else [done]))
         far.append(swapped(mine, "chan", top))
         near.append(fanned(mine))
         left.append(left_sides(mine))
-        ready = done
+        if p == last and paired:
+            far[0] = far[0][1]
+            result, done = cross(0, 1, arrived)
+            far[1:last] = [fanned(after(block, done)) for block in far[1:last]]
         result, done = cross(p, 0)
-        if p:
-            far[p - 1] = fanned(after(far[p - 1], ready) if p > 1 else far[p - 1])
+        if p == last and paired:
+            for n in range(1, last):
+                result, done = cross(n, 1)
+        if p == 0 and paired:
+            pieces = joined_pieces(own, parts, devices, begins[last], sizes[last], done)
+            far[0] = far[0], fanned(far[0])
+            pieces = [pieces[0]] + [swapped(pieces[d], "tm", d) for d in range(1, devices)]
+        if p and not paired:
+            far[p - 1] = fanned(far[p - 1])
             result, done = cross(p - 1, 1)
-    if not stacked:
-        far[-1] = fanned(after(far[-1], done))
-        result, _ = cross(len(chunks) - 1, 1)
+    far[-1] = fanned(after(far[-1], done))
+    result, _ = cross(last, 1)
     return result
 
 

time: 143 us -> 128 us (0.90)
  blocking collectives: 44.6 us -> 24.2 us
  starting transfers between devices: 15.7 us -> 31.9 us
  waiting for transfers between devices: 33.8 us -> 18.3 us
  local copies, waits for them, and re-layouts: 2.54 us -> 8.5 us
    all_to_all x2 -> x1, blocking collectives: 44.6 us -> 24.2 us  [exchanged(): return lax.all_to_all(chunk, 'tm', split_axis=0, concat_axis=0, tiled=True)]
    ppermute x9 -> x16, waiting for transfers between devices: 30.1 us -> 10.9 us  [swapped(): return lax.ppermute(shard, axis, [(i, i ^ bit) for i in range(devices)])]
    ppermute x9 -> x16, starting transfers between devices: 5.38 us -> 22 us  [swapped(): return lax.ppermute(shard, axis, [(i, i ^ bit) for i in range(devices)])]
    unnamed x10 -> x30, local copies, waits for them, and re-layouts: 2.54 us -> 8.5 us
    all_to_all x1, waiting for transfers between devices: 0.01 us -> 3.67 us  [exchanged(): return lax.all_to_all(chunk, 'tm', split_axis=0, concat_axis=0, tiled=True)]
  transfers between devices with their start and end apart: 12 -> 19, of which waited for: 5 -> 8; matrix products, arithmetic and copies ran while one was open for 0% -> 0% of each run, Pallas kernels for 26% -> 27%
where the time goes in v1:
time: 128 us; the launch traced here: 127 us
  Pallas kernels  44.4 us (35%)
  starting transfers between devices  31.9 us (25%)
  blocking collectives  24.2 us (19%)
  waiting for transfers between devices  18.3 us (14%)
  local copies, waits for them, and re-layouts  8.5 us (7%)
    all_to_all x1, blocking collectives, exchanged(): return lax.all_to_all(chunk, 'tm', split_axis=0, concat_axis=0, tiled=True)  24.2 us
    pallas_call x6, Pallas kernels, cross_products(): pl.pallas_call(functools.partial(cross_kernel, 2.0 / (sources * rows), si...  24.1 us
    ppermute x16, starting transfers between devices, swapped(): return lax.ppermute(shard, axis, [(i, i ^ bit) for i in range(devices)])  22 us
    ppermute x16, waiting for transfers between devices, swapped(): return lax.ppermute(shard, axis, [(i, i ^ bit) for i in range(devices)])  10.9 us
    pallas_call x1, Pallas kernels, own_spectra(): pl.pallas_call(spectra_kernel, out_shape=jax.ShapeDtypeStruct((BINS, 2 *...  10.2 us
    unnamed x30, local copies, waits for them, and re-layouts  8.5 us
    ppermute x2, starting transfers between devices, from_behind(): return lax.ppermute(shard, axis, pairs)  6.16 us
    ppermute x2, waiting for transfers between devices, from_behind(): return lax.ppermute(shard, axis, pairs)  3.76 us
  transfers between devices with their start and end apart: 19, of which 8 were waited for; matrix products, arithmetic and copies ran while one was open for 0% of the time, Pallas kernels for 27%

profile of v1, /device:TPU:0, one launch (start us, length us, event | category | flops | bytes accessed | tf_op | source)
XLA Modules:
  0.0 127.5 jit_solution(9634877473832725581)
XLA Ops:
  0.0 1.7 %outbox.1 = bf16[512,128]{1,0:T(8,128)(2,1)} custom-call(s32[16]{0:T(128)} %offsets.5, s32[16]{0:T(128)} %valid.3, f32[512,8192]{1,0:T(8,128)} %record.5), custom_call_target="tpu_custom_call" | custom-call | tf_op jit(solution)/shard_map/outbox/pallas_call | solution.py:87
  1.7 4.9 %collective-permute-start = (bf16[512,128]{1,0:T(8,128)(2,1)}, bf16[512,128]{1,0:T(8,128)(2,1)S(1)}, u32[]{:S(2)}, u32[]{:S(2)}) collective-permute-start(bf16[512,128]{1,0:T(8,128)(2,1)} %outbox.1), channel_id=1, source_target_pairs={{0,1},{1,2},{2,3},{3,4},{4,5},{5,6},{6,7},{8,9},{9,10},{10,11},{11... | collective-permute-start | bytes 393224 | tf_op jit(solution)/shard_map/ppermute | solution.py:31
  10.1 3.3 %border_parts.1 = (bf16[64,8,512]{2,1,0:T(8,128)(2,1)S(1)}, f32[8,128]{1,0:T(8,128)S(1)}) custom-call(bf16[512,128]{1,0:T(8,128)(2,1)S(1)} %collective-permute-done.inbox.rim, f32[512,8192]{1,0:T(8,128)} %record.5, bf16[2048,128]{1,0:T(8,128)(2,1)S(1)} %get-tuple-element.33.blocks, f32[384,128]{1,0:T(8,128)S(1)} %get-tuple-element.34.rise, ...), custom_call_target="tpu_custom_call" | custom-call | flops 402653184 | bytes 3670016 | tf_op jit(solution)/shard_map/border_parts/pallas_call | solution.py:183
  14.7 10.2 %own_spectra.1.own = bf16[64,32,512]{2,1,0:T(8,128)(2,1)S(1)} custom-call(s32[16]{0:T(128)S(1)} %copy-done.7, s32[16]{0:T(128)S(1)} %copy-done.8, f32[512,8192]{1,0:T(8,128)} %record.5, bf16[512,128]{1,0:T(8,128)(2,1)S(1)} %collective-permute-done.inbox.rim, bf16[2048,128]{1,0:T(8,128)(2,1)S(1)} %get-tuple-element.33.blocks, ...), custom_call_target="tpu_custom_call" | custom-call | flops 1879048192 | bytes 16777216 | tf_op jit(solution)/shard_map/own_spectra/pallas_call | solution.py:269
  24.9 3.8 %collective-permute-done.1.parts = bf16[64,8,512]{2,1,0:T(8,128)(2,1)S(1)} collective-permute-done((bf16[64,8,512]{2,1,0:T(8,128)(2,1)S(1)}, bf16[64,8,512]{2,1,0:T(8,128)(2,1)S(1)}, u32[]{:S(2)}, u32[]{:S(2)}) %collective-permute-start.1) | collective-permute-done | bytes 524320 | tf_op jit(solution)/shard_map/ppermute | solution.py:31
  28.9 24.2 %all_to_all.10.own.rest_0_ = bf16[8,3,32,512]{3,2,1,0:T(8,128)(2,1)} all-to-all(bf16[8,3,32,512]{3,2,1,0:T(8,128)(2,1)S(1)} %get-tuple-element.39), channel_id=1, replica_groups=mesh['chan'=4,'tm'=8] {'tm'}, dimensions={0} | all-to-all | bytes 1572864 | tf_op jit(solution)/shard_map/all_to_all | solution.py:504
  53.1 3.7 %all-to-all-start.1 = ((bf16[8,3,32,512]{3,2,1,0:T(8,128)(2,1)}), bf16[8,3,32,512]{3,2,1,0:T(8,128)(2,1)S(1)}, u32[]{:S(2)}, u32[]{:S(2)}) async-start(bf16[8,3,32,512]{3,2,1,0:T(8,128)(2,1)} %copy-done.5), calls=%async_computation.1 | async-start | bytes 1572864 | tf_op jit(solution)/shard_map/all_to_all | solution.py:504
  56.9 1.5 %collective-permute-start.10 = (bf16[8,3,32,512]{3,2,1,0:T(8,128)(2,1)}, bf16[8,3,32,512]{3,2,1,0:T(8,128)(2,1)}, u32[]{:S(2)}, u32[]{:S(2)}) collective-permute-start(bf16[8,3,32,512]{3,2,1,0:T(8,128)(2,1)} %all_to_all.10.own.rest_0_), channel_id=1, source_target_pairs={{0,16},{8,24},{16,0},{24,8},{1,17},{9,25},{17,1},{25,9},{2,18},{10... | collective-permute-start | bytes 2359304 | tf_op jit(solution)/shard_map/ppermute | solution.py:467
  60.4 1.7 %copy-done.3 = bf16[8,3,32,512]{3,2,1,0:T(8,128)(2,1)S(1)} copy-done((bf16[8,3,32,512]{3,2,1,0:T(8,128)(2,1)S(1)}, bf16[8,3,32,512]{3,2,1,0:T(8,128)(2,1)}, u32[]{:S(2)}) %copy-start.3) | copy-done | bytes 786456
  62.1 5.0 %cross_products.6 = (bf16[8,2,512,2048]{3,2,1,0:T(8,128)(2,1)}, f32[8,128]{1,0:T(8,128)S(1)}) custom-call(s32[1]{0:T(128)} %bitcast.me, bf16[3,1024,256]{2,1,0:T(8,128)(2,1)S(1)} %left_sides.3.left.rest_2_, bf16[8,3,32,512]{3,2,1,0:T(8,128)(2,1)S(1)} %copy-done.3, bf16[8,3,32,512]{3,2,1,0:T(8,128)(2,1)} %collective-permute-done.2.rest_1_, ...), custom_call_target="tpu_custom_call" | custom-call | flops 1610612736 | bytes 6291456 | tf_op jit(solution)/shard_map/cross_products/pallas_call | solution.py:442
  70.9 1.7 %collective-permute-start.3 = (bf16[2,32,512]{2,1,0:T(8,128)(2,1)}, bf16[2,32,512]{2,1,0:T(8,128)(2,1)S(1)}, u32[]{:S(2)}, u32[]{:S(2)}) collective-permute-start(bf16[2,32,512]{2,1,0:T(8,128)(2,1)} %get-tuple-element.42), channel_id=1, source_target_pairs={{0,1},{1,0},{2,3},{3,2},{4,5},{5,4},{6,7},{7,6},{8,9},{9,8},{10,11... | collective-permute-start | bytes 196616 | tf_op jit(solution)/shard_map/ppermute | solution.py:467
  72.6 3.7 %all-to-all-done.1.shard = bf16[8,3,32,512]{3,2,1,0:T(8,128)(2,1)S(1)} async-done(((bf16[8,3,32,512]{3,2,1,0:T(8,128)(2,1)}), bf16[8,3,32,512]{3,2,1,0:T(8,128)(2,1)S(1)}, u32[]{:S(2)}, u32[]{:S(2)}) %all-to-all-start.1) | async-done | bytes 786464 | tf_op jit(solution)/shard_map/all_to_all | solution.py:504
  80.4 1.8 %collective-permute-start.4 = (bf16[2,32,512]{2,1,0:T(8,128)(2,1)}, bf16[2,32,512]{2,1,0:T(8,128)(2,1)S(1)}, u32[]{:S(2)}, u32[]{:S(2)}) collective-permute-start(bf16[2,32,512]{2,1,0:T(8,128)(2,1)} %copy-done.14), channel_id=1, source_target_pairs={{0,2},{1,3},{2,0},{3,1},{4,6},{5,7},{6,4},{7,5},{8,10},{9,11},{10,... | collective-permute-start | bytes 196616 | tf_op jit(solution)/shard_map/ppermute | solution.py:467
  85.0 2.6 %collective-permute-start.6 = (bf16[2,32,512]{2,1,0:T(8,128)(2,1)}, bf16[2,32,512]{2,1,0:T(8,128)(2,1)S(1)}, u32[]{:S(2)}, u32[]{:S(2)}) collective-permute-start(bf16[2,32,512]{2,1,0:T(8,128)(2,1)} %copy-done.12), channel_id=1, source_target_pairs={{0,4},{1,5},{2,6},{3,7},{4,0},{5,1},{6,2},{7,3},{8,12},{9,13},{10,... | collective-permute-start | bytes 196616 | tf_op jit(solution)/shard_map/ppermute | solution.py:467
  88.3 3.1 %collective-permute-start.7 = (bf16[2,32,512]{2,1,0:T(8,128)(2,1)}, bf16[2,32,512]{2,1,0:T(8,128)(2,1)S(1)}, u32[]{:S(2)}, u32[]{:S(2)}) collective-permute-start(bf16[2,32,512]{2,1,0:T(8,128)(2,1)} %copy-done.11), channel_id=1, source_target_pairs={{0,5},{1,4},{2,7},{3,6},{4,1},{5,0},{6,3},{7,2},{8,13},{9,12},{10,... | collective-permute-start | bytes 196616 | tf_op jit(solution)/shard_map/ppermute | solution.py:467
  91.5 4.5 %collective-permute-start.8 = (bf16[2,32,512]{2,1,0:T(8,128)(2,1)}, bf16[2,32,512]{2,1,0:T(8,128)(2,1)S(1)}, u32[]{:S(2)}, u32[]{:S(2)}) collective-permute-start(bf16[2,32,512]{2,1,0:T(8,128)(2,1)} %copy-done.10), channel_id=1, source_target_pairs={{0,6},{1,7},{2,4},{3,5},{4,2},{5,3},{6,0},{7,1},{8,14},{9,15},{10,... | collective-permute-start | bytes 196616 | tf_op jit(solution)/shard_map/ppermute | solution.py:467
  96.0 1.9 %collective-permute-start.9 = (bf16[2,32,512]{2,1,0:T(8,128)(2,1)S(1)}, bf16[2,32,512]{2,1,0:T(8,128)(2,1)S(1)}, u32[]{:S(2)}, u32[]{:S(2)}) collective-permute-start(bf16[2,32,512]{2,1,0:T(8,128)(2,1)S(1)} %get-tuple-element.48), channel_id=1, source_target_pairs={{0,7},{1,6},{2,5},{3,4},{4,3},{5,2},{6,1},{7,0},{8,15},{9,14},{10,... | collective-permute-start | bytes 196616 | tf_op jit(solution)/shard_map/ppermute | solution.py:467
  98.0 4.2 %cross_products.7 = (bf16[8,2,512,2048]{3,2,1,0:T(8,128)(2,1)}, f32[8,128]{1,0:T(8,128)S(1)}) custom-call(s32[1]{0:T(128)} %bitcast.me, bf16[3,1024,256]{2,1,0:T(8,128)(2,1)S(1)} %left_sides.4.left, bf16[8,3,32,512]{3,2,1,0:T(8,128)(2,1)S(1)} %after.3.own.rest_0_, ...), custom_call_target="tpu_custom_call", output_to_operand_aliasing={{0}: (4, {})} | custom-call | flops 1610612736 | bytes 6291456 | tf_op jit(solution)/shard_map/cross_products/pallas_call | solution.py:442
  103.0 5.0 %cross_products.8 = (bf16[8,2,512,2048]{3,2,1,0:T(8,128)(2,1)}, f32[8,128]{1,0:T(8,128)S(1)}) custom-call(s32[1]{0:T(128)} %bitcast.me, bf16[3,1024,256]{2,1,0:T(8,128)(2,1)S(1)} %copy-done.1, bf16[8,3,32,512]{3,2,1,0:T(8,128)(2,1)} %collective-permute-done.10.refs_1_.rest_0_, ...), custom_call_target="tpu_custom_call", output_to_operand_aliasing={{0}: (4, {})} | custom-call | flops 1610612736 | bytes 6291456 | tf_op jit(solution)/shard_map/cross_products/pallas_call | solution.py:442
  111.2 2.9 %cross_products.9 = (bf16[8,2,512,2048]{3,2,1,0:T(8,128)(2,1)}, f32[8,128]{1,0:T(8,128)}) custom-call(s32[1]{0:T(128)} %bitcast.me, bf16[2,1024,256]{2,1,0:T(8,128)(2,1)S(1)} %left_sides.5.left, bf16[8,2,32,512]{3,2,1,0:T(8,128)(2,1)S(1)} %get-tuple-element.52.own.rest_0_, ...), custom_call_target="tpu_custom_call", output_to_operand_aliasing={{0}: (4, {})} | custom-call | flops 1073741824 | bytes 4194304 | tf_op jit(solution)/shard_map/cross_products/pallas_call | solution.py:442
  114.1 4.2 %cross_products.10 = (bf16[8,2,512,2048]{3,2,1,0:T(8,128)(2,1)}, f32[8,128]{1,0:T(8,128)S(1)}) custom-call(s32[1]{0:T(128)} %bitcast.me, bf16[3,1024,256]{2,1,0:T(8,128)(2,1)S(1)} %left_sides.4.left, bf16[8,3,32,512]{3,2,1,0:T(8,128)(2,1)S(1)} %after.4.rest_0_, ...), custom_call_target="tpu_custom_call", output_to_operand_aliasing={{0}: (4, {})} | custom-call | flops 1610612736 | bytes 6291456 | tf_op jit(solution)/shard_map/cross_products/pallas_call | solution.py:442
  118.3 4.4 %collective-permute-done.12.shard = bf16[8,2,32,512]{3,2,1,0:T(8,128)(2,1)S(1)} collective-permute-done((bf16[8,2,32,512]{3,2,1,0:T(8,128)(2,1)S(1)}, bf16[8,2,32,512]{3,2,1,0:T(8,128)(2,1)S(1)}, u32[]{:S(2)}, u32[]{:S(2)}) %collective-permute-start.12) | collective-permute-done | bytes 524320 | tf_op jit(solution)/shard_map/ppermute | solution.py:467
  122.7 1.9 %collective-permute-done.17.rest_1_ = bf16[8,2,32,512]{3,2,1,0:T(8,128)(2,1)S(1)} collective-permute-done((bf16[8,2,32,512]{3,2,1,0:T(8,128)(2,1)S(1)}, bf16[8,2,32,512]{3,2,1,0:T(8,128)(2,1)S(1)}, u32[]{:S(2)}, u32[]{:S(2)}) %collective-permute-start.17) | collective-permute-done | bytes 524320 | tf_op jit(solution)/shard_map/ppermute | solution.py:467
  124.6 2.9 %cross_products.11 = (bf16[8,2,512,2048]{3,2,1,0:T(8,128)(2,1)}, f32[8,128]{1,0:T(8,128)}) custom-call(s32[1]{0:T(128)} %bitcast.me, bf16[2,1024,256]{2,1,0:T(8,128)(2,1)S(1)} %left_sides.5.left, bf16[8,2,32,512]{3,2,1,0:T(8,128)(2,1)S(1)} %after.5.rest_0_, ...), custom_call_target="tpu_custom_call", output_to_operand_aliasing={{0}: (4, {})} | custom-call | flops 1073741824 | bytes 4194304 | tf_op jit(solution)/shard_map/cross_products/pallas_call | solution.py:442
  (64 shorter events, 22.6 us)
Async XLA Ops:
  0.0 14.7 %copy-start.7 = (s32[16]{0:T(128)S(1)}, s32[16]{0:T(128)}, u32[]{:S(2)}) copy-start(s32[16]{0:T(128)} %offsets.5) | copy-start | bytes 196
  0.0 14.7 %copy-start.8 = (s32[16]{0:T(128)S(1)}, s32[16]{0:T(128)}, u32[]{:S(2)}) copy-start(s32[16]{0:T(128)} %valid.3) | copy-start | bytes 196
  1.7 8.4 %collective-permute-start = (bf16[512,128]{1,0:T(8,128)(2,1)}, bf16[512,128]{1,0:T(8,128)(2,1)S(1)}, u32[]{:S(2)}, u32[]{:S(2)}) collective-permute-start(bf16[512,128]{1,0:T(8,128)(2,1)} %outbox.1), channel_id=1, source_target_pairs={{0,1},{1,2},{2,3},{3,4},{4,5},{5,6},{6,7},{8,9},{9,10},{10,11},{11... | collective-permute-start | bytes 393224 | tf_op jit(solution)/shard_map/ppermute | solution.py:31
  13.4 15.3 %collective-permute-start.1 = (bf16[64,8,512]{2,1,0:T(8,128)(2,1)S(1)}, bf16[64,8,512]{2,1,0:T(8,128)(2,1)S(1)}, u32[]{:S(2)}, u32[]{:S(2)}) collective-permute-start(bf16[64,8,512]{2,1,0:T(8,128)(2,1)S(1)} %get-tuple-element.38), channel_id=1, source_target_pairs={{1,0},{2,1},{3,2},{4,3},{5,4},{6,5},{7,6},{9,8},{10,9},{11,10},{12... | collective-permute-start | bytes 1572872 | tf_op jit(solution)/shard_map/ppermute | solution.py:31
  28.9 24.2 %copy-start.5 = (bf16[8,3,32,512]{3,2,1,0:T(8,128)(2,1)}, bf16[8,3,32,512]{3,2,1,0:T(8,128)(2,1)S(1)}, u32[]{:S(2)}) copy-start(bf16[8,3,32,512]{3,2,1,0:T(8,128)(2,1)S(1)} %get-tuple-element.49) | copy-start | bytes 2359300
  53.1 23.2 %all-to-all-start.1 = ((bf16[8,3,32,512]{3,2,1,0:T(8,128)(2,1)}), bf16[8,3,32,512]{3,2,1,0:T(8,128)(2,1)S(1)}, u32[]{:S(2)}, u32[]{:S(2)}) async-start(bf16[8,3,32,512]{3,2,1,0:T(8,128)(2,1)} %copy-done.5), calls=%async_computation.1 | async-start | bytes 1572864 | tf_op jit(solution)/shard_map/all_to_all | solution.py:504
  56.8 3.5 %collective-permute-start.2 = (bf16[8,3,32,512]{3,2,1,0:T(8,128)(2,1)}, bf16[8,3,32,512]{3,2,1,0:T(8,128)(2,1)}, u32[]{:S(2)}, u32[]{:S(2)}) collective-permute-start(bf16[8,3,32,512]{3,2,1,0:T(8,128)(2,1)} %all_to_all.10.own.rest_0_), channel_id=1, source_target_pairs={{0,8},{8,0},{16,24},{24,16},{1,9},{9,1},{17,25},{25,17},{2,10},{10... | collective-permute-start | bytes 2359304 | tf_op jit(solution)/shard_map/ppermute | solution.py:467
  56.9 20.3 %collective-permute-start.10 = (bf16[8,3,32,512]{3,2,1,0:T(8,128)(2,1)}, bf16[8,3,32,512]{3,2,1,0:T(8,128)(2,1)}, u32[]{:S(2)}, u32[]{:S(2)}) collective-permute-start(bf16[8,3,32,512]{3,2,1,0:T(8,128)(2,1)} %all_to_all.10.own.rest_0_), channel_id=1, source_target_pairs={{0,16},{8,24},{16,0},{24,8},{1,17},{9,25},{17,1},{25,9},{2,18},{10... | collective-permute-start | bytes 2359304 | tf_op jit(solution)/shard_map/ppermute | solution.py:467
  60.4 7.4 %copy-start = (bf16[3,1024,256]{2,1,0:T(8,128)(2,1)}, bf16[3,1024,256]{2,1,0:T(8,128)(2,1)S(1)}, u32[]{:S(2)}) copy-start(bf16[3,1024,256]{2,1,0:T(8,128)(2,1)S(1)} %left_sides.3.left.rest_2_) | copy-start | bytes 4718596
  70.9 32.2 %copy-start.1 = (bf16[3,1024,256]{2,1,0:T(8,128)(2,1)S(1)}, bf16[3,1024,256]{2,1,0:T(8,128)(2,1)}, u32[]{:S(2)}) copy-start(bf16[3,1024,256]{2,1,0:T(8,128)(2,1)} %copy-done) | copy-start | bytes 4718596
  70.9 6.3 %collective-permute-start.3 = (bf16[2,32,512]{2,1,0:T(8,128)(2,1)}, bf16[2,32,512]{2,1,0:T(8,128)(2,1)S(1)}, u32[]{:S(2)}, u32[]{:S(2)}) collective-permute-start(bf16[2,32,512]{2,1,0:T(8,128)(2,1)} %get-tuple-element.42), channel_id=1, source_target_pairs={{0,1},{1,0},{2,3},{3,2},{4,5},{5,4},{6,7},{7,6},{8,9},{9,8},{10,11... | collective-permute-start | bytes 196616 | tf_op jit(solution)/shard_map/ppermute | solution.py:467
  78.4 17.6 %collective-permute-start.11 = (bf16[8,3,32,512]{3,2,1,0:T(8,128)(2,1)S(1)}, bf16[8,3,32,512]{3,2,1,0:T(8,128)(2,1)S(1)}, u32[]{:S(2)}, u32[]{:S(2)}) collective-permute-start(bf16[8,3,32,512]{3,2,1,0:T(8,128)(2,1)S(1)} %after.3.own.rest_0_), channel_id=1, source_target_pairs={{0,8},{8,0},{16,24},{24,16},{1,9},{9,1},{17,25},{25,17},{2,10},{10... | collective-permute-start | bytes 2359304 | tf_op jit(solution)/shard_map/ppermute | solution.py:467
  78.5 24.6 %collective-permute-start.14 = (bf16[8,3,32,512]{3,2,1,0:T(8,128)(2,1)}, bf16[8,3,32,512]{3,2,1,0:T(8,128)(2,1)S(1)}, u32[]{:S(2)}, u32[]{:S(2)}) collective-permute-start(bf16[8,3,32,512]{3,2,1,0:T(8,128)(2,1)} %collective-permute-done.10.refs_1_.rest_0_), channel_id=1, source_target_pairs={{0,8},{8,0},{16,24},{24,16},{1,9},{9,1},{17,25},{25,17},{2,10},{10... | collective-permute-start | bytes 2359304 | tf_op jit(solution)/shard_map/ppermute | solution.py:467
  79.0 29.1 %collective-permute-start.13 = (bf16[8,3,32,512]{3,2,1,0:T(8,128)(2,1)S(1)}, bf16[8,3,32,512]{3,2,1,0:T(8,128)(2,1)S(1)}, u32[]{:S(2)}, u32[]{:S(2)}) collective-permute-start(bf16[8,3,32,512]{3,2,1,0:T(8,128)(2,1)S(1)} %after.3.own.rest_0_), channel_id=1, source_target_pairs={{0,16},{8,24},{16,0},{24,8},{1,17},{9,25},{17,1},{25,9},{2,18},{10... | collective-permute-start | bytes 2359304 | tf_op jit(solution)/shard_map/ppermute | solution.py:467
  80.4 4.6 %collective-permute-start.4 = (bf16[2,32,512]{2,1,0:T(8,128)(2,1)}, bf16[2,32,512]{2,1,0:T(8,128)(2,1)S(1)}, u32[]{:S(2)}, u32[]{:S(2)}) collective-permute-start(bf16[2,32,512]{2,1,0:T(8,128)(2,1)} %copy-done.14), channel_id=1, source_target_pairs={{0,2},{1,3},{2,0},{3,1},{4,6},{5,7},{6,4},{7,5},{8,10},{9,11},{10,... | collective-permute-start | bytes 196616 | tf_op jit(solution)/shard_map/ppermute | solution.py:467
  82.2 6.1 %collective-permute-start.5 = (bf16[2,32,512]{2,1,0:T(8,128)(2,1)}, bf16[2,32,512]{2,1,0:T(8,128)(2,1)S(1)}, u32[]{:S(2)}, u32[]{:S(2)}) collective-permute-start(bf16[2,32,512]{2,1,0:T(8,128)(2,1)} %copy-done.13), channel_id=1, source_target_pairs={{0,3},{1,2},{2,1},{3,0},{4,7},{5,6},{6,5},{7,4},{8,11},{9,10},{10,... | collective-permute-start | bytes 196616 | tf_op jit(solution)/shard_map/ppermute | solution.py:467
  85.0 6.5 %collective-permute-start.6 = (bf16[2,32,512]{2,1,0:T(8,128)(2,1)}, bf16[2,32,512]{2,1,0:T(8,128)(2,1)S(1)}, u32[]{:S(2)}, u32[]{:S(2)}) collective-permute-start(bf16[2,32,512]{2,1,0:T(8,128)(2,1)} %copy-done.12), channel_id=1, source_target_pairs={{0,4},{1,5},{2,6},{3,7},{4,0},{5,1},{6,2},{7,3},{8,12},{9,13},{10,... | collective-permute-start | bytes 196616 | tf_op jit(solution)/shard_map/ppermute | solution.py:467
  88.3 13.8 %collective-permute-start.7 = (bf16[2,32,512]{2,1,0:T(8,128)(2,1)}, bf16[2,32,512]{2,1,0:T(8,128)(2,1)S(1)}, u32[]{:S(2)}, u32[]{:S(2)}) collective-permute-start(bf16[2,32,512]{2,1,0:T(8,128)(2,1)} %copy-done.11), channel_id=1, source_target_pairs={{0,5},{1,4},{2,7},{3,6},{4,1},{5,0},{6,3},{7,2},{8,13},{9,12},{10,... | collective-permute-start | bytes 196616 | tf_op jit(solution)/shard_map/ppermute | solution.py:467
  91.5 10.6 %collective-permute-start.8 = (bf16[2,32,512]{2,1,0:T(8,128)(2,1)}, bf16[2,32,512]{2,1,0:T(8,128)(2,1)S(1)}, u32[]{:S(2)}, u32[]{:S(2)}) collective-permute-start(bf16[2,32,512]{2,1,0:T(8,128)(2,1)} %copy-done.10), channel_id=1, source_target_pairs={{0,6},{1,7},{2,4},{3,5},{4,2},{5,3},{6,0},{7,1},{8,14},{9,15},{10,... | collective-permute-start | bytes 196616 | tf_op jit(solution)/shard_map/ppermute | solution.py:467
  96.0 7.0 %collective-permute-start.9 = (bf16[2,32,512]{2,1,0:T(8,128)(2,1)S(1)}, bf16[2,32,512]{2,1,0:T(8,128)(2,1)S(1)}, u32[]{:S(2)}, u32[]{:S(2)}) collective-permute-start(bf16[2,32,512]{2,1,0:T(8,128)(2,1)S(1)} %get-tuple-element.48), channel_id=1, source_target_pairs={{0,7},{1,6},{2,5},{3,4},{4,3},{5,2},{6,1},{7,0},{8,15},{9,14},{10,... | collective-permute-start | bytes 196616 | tf_op jit(solution)/shard_map/ppermute | solution.py:467
  108.1 6.0 %collective-permute-start.15 = (bf16[8,3,32,512]{3,2,1,0:T(8,128)(2,1)S(1)}, bf16[8,3,32,512]{3,2,1,0:T(8,128)(2,1)S(1)}, u32[]{:S(2)}, u32[]{:S(2)}) collective-permute-start(bf16[8,3,32,512]{3,2,1,0:T(8,128)(2,1)S(1)} %after.4.rest_0_), channel_id=1, source_target_pairs={{0,8},{8,0},{16,24},{24,16},{1,9},{9,1},{17,25},{25,17},{2,10},{10... | collective-permute-start | bytes 2359304 | tf_op jit(solution)/shard_map/ppermute | solution.py:467
  108.2 3.0 %collective-permute-start.16 = (bf16[8,2,32,512]{3,2,1,0:T(8,128)(2,1)S(1)}, bf16[8,2,32,512]{3,2,1,0:T(8,128)(2,1)S(1)}, u32[]{:S(2)}, u32[]{:S(2)}) collective-permute-start(bf16[8,2,32,512]{3,2,1,0:T(8,128)(2,1)S(1)} %get-tuple-element.52.own.rest_0_), channel_id=1, source_target_pairs={{0,8},{8,0},{16,24},{24,16},{1,9},{9,1},{17,25},{25,17},{2,10},{10... | collective-permute-start | bytes 1572872 | tf_op jit(solution)/shard_map/ppermute | solution.py:467
  108.7 13.9 %collective-permute-start.12 = (bf16[8,2,32,512]{3,2,1,0:T(8,128)(2,1)S(1)}, bf16[8,2,32,512]{3,2,1,0:T(8,128)(2,1)S(1)}, u32[]{:S(2)}, u32[]{:S(2)}) collective-permute-start(bf16[8,2,32,512]{3,2,1,0:T(8,128)(2,1)S(1)} %get-tuple-element.52.own.rest_0_), channel_id=1, source_target_pairs={{0,16},{8,24},{16,0},{24,8},{1,17},{9,25},{17,1},{25,9},{2,18},{10... | collective-permute-start | bytes 1572872 | tf_op jit(solution)/shard_map/ppermute | solution.py:467
  122.7 2.0 %collective-permute-start.17 = (bf16[8,2,32,512]{3,2,1,0:T(8,128)(2,1)S(1)}, bf16[8,2,32,512]{3,2,1,0:T(8,128)(2,1)S(1)}, u32[]{:S(2)}, u32[]{:S(2)}) collective-permute-start(bf16[8,2,32,512]{3,2,1,0:T(8,128)(2,1)S(1)} %after.5.rest_0_), channel_id=1, source_target_pairs={{0,8},{8,0},{16,24},{24,16},{1,9},{9,1},{17,25},{25,17},{2,10},{10... | collective-permute-start | bytes 1572872 | tf_op jit(solution)/shard_map/ppermute | solution.py:467
  (10 other events, 8.5 us)
